TPU v7x, 32 devices: a whole 2x2x4 slice. The times are simulated.
32 devices in a mesh: seq: 8 (over z, x), mp: 4 (over y, core).
Axes of the slice: x: 2, y: 2, z: 4, core: 2. Of those that a mesh axis runs over, the one named last changes fastest.
Arguments:
- fields_in: bfloat16 [2048, 3, 4096], P('seq', None, 'mp'), may hold values from -6 to 6
- pack_source: int32 [2048], P('seq'), may hold values from 0 to 2047, as said below
- doc_start: int32 [2048], P('seq'), may hold values from 0 to 2047, as said below
- short_filter: float32 [3, 3, 4096], P(None, None, 'mp'), may hold values from -2.4 to 2.4
- memory: float32 [2, 4096], P(None, 'mp'), may hold values from 30 to 8192
- residue: float32 [2, 4096], P(None, 'mp'), may hold values from -4 to 4
- skip_gain: float32 [4096], P('mp'), may hold values from -2.5 to 2.5
- w_out: bfloat16 [4096, 4096], P('mp'), may hold values from -0.09375 to 0.09375
- cotangent: bfloat16 [2048, 4096], P('seq', 'mp'), may hold values from -6 to 6
Outputs:
- mixed: bfloat16 [2048, 4096], P('seq', 'mp')
- d_fields: bfloat16 [2048, 3, 4096], P('seq', None, 'mp')
- d_filter: float32 [3, 3, 4096], P(None, None, 'mp')
- d_residue: float32 [2, 4096], P(None, 'mp')
- d_skip: float32 [4096], P('mp')
Inputs may be any that keep to these rules, and one draw needn't show every extreme that they name: pack_source is a permutation of the 2048 loader rows. Of the 256 positions of one aligned block, at most 64 take rows of one and the same aligned block of loader rows, and in every draw some pair of blocks reaches 64. doc_start[t] is the first position of the document that holds position t; documents are runs of consecutive positions, and the longest has exactly 1024 positions.
All inputs are finite; a program needn't handle non-finite values.
Results may differ from a plain program's by a relative error of at most 0.0049.
Values may be sent and summed in bfloat16 or wider, within the bound.
A program may use at most 256 MiB of HBM per device.

v0:
```python
import jax
import jax.numpy as jnp
from jax import lax
from jax.experimental import pallas as pl
from jax.experimental.pallas import tpu as pltpu
from jax.sharding import PartitionSpec as P


def shifted(shard, axis, by):
    peers = lax.axis_size(axis)
    pairs = [(i, i + by) for i in range(peers) if 0 <= i + by < peers]
    return lax.ppermute(shard, axis, pairs)


def compose(earlier, later):
    return (earlier[0] * later[0], later[0] * earlier[1] + later[1])


def forward_scan(links, source, axis):
    return lax.associative_scan(compose, (links, source), axis=axis)


def backward_scan(links, source, axis):
    length = links.shape[axis]
    ahead = jnp.concatenate(
        [
            lax.slice_in_dim(links, 1, length, axis=axis),
            jnp.ones_like(lax.slice_in_dim(links, 0, 1, axis=axis)),
        ],
        axis=axis,
    )
    flipped = forward_scan(jnp.flip(ahead, axis), jnp.flip(source, axis), axis)
    return (jnp.flip(flipped[0], axis), jnp.flip(flipped[1], axis))


def rows_of(array, chosen_rows):
    flat = array.reshape(array.shape[0], -1)
    picked = jnp.dot(chosen_rows.astype(array.dtype), flat, preferred_element_type=jnp.float32)
    return picked.astype(array.dtype).reshape((-1,) + array.shape[1:])


def per_device(
    fields_in, pack_source, doc_start, short_filter, memory, residue, skip_gain, w_out, cotangent
):
    rows = fields_in.shape[0]
    width = fields_in.shape[2]
    devices_seq = lax.axis_size("seq")
    here = lax.axis_index("seq")
    capacity = 2 * rows // devices_seq
    source_dev = pack_source // rows
    source_row = pack_source % rows
    line = jnp.arange(rows, dtype=jnp.int32)
    before = (line[:, None] > line[None, :]) & (source_dev[:, None] == source_dev[None, :])
    slot = source_dev * capacity + jnp.sum(before.astype(jnp.int32), axis=1)
    filled = jnp.arange(devices_seq * capacity, dtype=jnp.int32)[:, None] == slot[None, :]
    wanted = jnp.min(jnp.where(filled, source_row[None, :], rows), axis=1)
    wanted = wanted.reshape(devices_seq, capacity)
    asked = lax.all_to_all(wanted, "seq", split_axis=0, concat_axis=0, tiled=True)
    picked = rows_of(fields_in, asked.reshape(-1)[:, None] == line[None, :]).reshape(
        asked.shape[0], asked.shape[1], 3, width
    )
    returned_rows = lax.all_to_all(picked, "seq", split_axis=0, concat_axis=0, tiled=True)
    packed = rows_of(returned_rows.reshape(devices_seq * capacity, 3, width), filled.T)
    position = here * rows + line
    masks = [(position - lag >= doc_start).astype(jnp.float32)[:, None, None] for lag in range(3)]
    tail = shifted(packed[rows - 2 :], "seq", 1)
    extended = jnp.concatenate([tail, packed], axis=0).astype(jnp.float32)
    lagged = [extended[2 - lag : 2 - lag + rows] for lag in range(3)]
    short = masks[0] * short_filter[None, :, 0, :] * lagged[0]
    for lag in (1, 2):
        short = short + masks[lag] * short_filter[None, :, lag, :] * lagged[lag]
    query = short[:, 0]
    keys_part = short[:, 1]
    values_part = short[:, 2]
    drive = keys_part * values_part
    decay = jnp.exp(-1.0 / memory)
    norm_gain = jnp.sqrt(1.0 - decay * decay)
    mode_gain = residue * norm_gain
    part_width = width // devices_seq
    bounds = lax.all_gather(doc_start, "seq", axis=0, tiled=True)
    everywhere = jnp.arange(bounds.shape[0], dtype=jnp.int32)
    link_all = (bounds < everywhere).astype(jnp.float32)
    decay_part = lax.dynamic_slice_in_dim(decay, here * part_width, part_width, 1)
    gain_part = lax.dynamic_slice_in_dim(mode_gain, here * part_width, part_width, 1)
    norm_part = lax.dynamic_slice_in_dim(norm_gain, here * part_width, part_width, 1)
    skip_part = lax.dynamic_slice_in_dim(skip_gain, here * part_width, part_width, 0)
    drive_part = lax.all_to_all(drive.T, "seq", split_axis=0, concat_axis=1, tiled=True)
    links_part = decay_part[:, :, None] * link_all[None, None, :]
    state_part = forward_scan(links_part, jnp.broadcast_to(drive_part[None], links_part.shape), 2)[
        1
    ]
    filtered_part = (
        jnp.sum(gain_part[:, :, None] * state_part, axis=0) + skip_part[:, None] * drive_part
    )
    filtered = lax.all_to_all(filtered_part, "seq", split_axis=1, concat_axis=0, tiled=True).T
    gated = (query * filtered).astype(jnp.bfloat16)
    partial_out = jnp.dot(gated, w_out, preferred_element_type=jnp.float32)
    mixed = lax.psum_scatter(partial_out, "mp", scatter_dimension=1, tiled=True).astype(
        jnp.bfloat16
    )
    d_gated = lax.dot_general(
        lax.all_gather(cotangent, "mp", axis=1, tiled=True),
        w_out,
        (((1,), (1,)), ((), ())),
        preferred_element_type=jnp.float32,
    )
    d_query = d_gated * filtered
    d_filtered = d_gated * query
    grad_part = lax.all_to_all(d_filtered.T, "seq", split_axis=0, concat_axis=1, tiled=True)
    adjoint_part = backward_scan(links_part, gain_part[:, :, None] * grad_part[None], 2)[1]
    back_part = jnp.sum(adjoint_part, axis=0)
    d_drive = (
        skip_gain[None] * d_filtered
        + lax.all_to_all(back_part, "seq", split_axis=1, concat_axis=0, tiled=True).T
    )
    residue_part = norm_part * jnp.sum(grad_part[None] * state_part, axis=2)
    d_residue = lax.all_gather(residue_part, "seq", axis=1, tiled=True)
    d_short = jnp.stack([d_query, d_drive * values_part, d_drive * keys_part], axis=1)
    weighted = [d_short * masks[lag] for lag in range(3)]
    head = jnp.stack(
        [
            short_filter[:, 2, :] * weighted[2][0],
            short_filter[:, 1, :] * weighted[1][0] + short_filter[:, 2, :] * weighted[2][1],
        ],
        axis=0,
    )
    from_next = shifted(head, "seq", -1)
    zero_row = jnp.zeros((1, 3, width), jnp.float32)
    d_packed = short_filter[None, :, 0, :] * weighted[0]
    d_packed = d_packed + short_filter[None, :, 1, :] * jnp.concatenate(
        [weighted[1][1:], zero_row], axis=0
    )
    d_packed = d_packed + short_filter[None, :, 2, :] * jnp.concatenate(
        [weighted[2][2:], zero_row, zero_row], axis=0
    )
    d_packed = d_packed + jnp.concatenate(
        [jnp.zeros((rows - 2, 3, width), jnp.float32), from_next], axis=0
    )
    filter_local = jnp.stack(
        [jnp.sum(weighted[lag] * lagged[lag], axis=0) for lag in range(3)], axis=1
    )
    skip_local = jnp.sum(d_filtered * drive, axis=0)
    d_filter, d_skip = lax.psum((filter_local, skip_local), "seq")
    outgoing = (
        rows_of(d_packed.astype(jnp.bfloat16), filled).reshape(devices_seq, capacity, 3, width)
    )
    returned = lax.all_to_all(outgoing, "seq", split_axis=0, concat_axis=0, tiled=True)
    d_fields = rows_of(returned.reshape(-1, 3, width), line[:, None] == asked.reshape(-1)[None, :])
    return (mixed, d_fields, d_filter, d_residue, d_skip)


PAD = 8
SEGS = 32
LANES = 128


def channel_kernel(
    x_ref, dg_ref, src_col_ref, src_row_ref, rel_ref, taps_ref, memory_ref, residue_ref, skip_ref,
    gated_ref, d_fields_ref, sums_ref,
    x_s, ds_s, dg_s, gated_s, drive_s, k_s, v_s, df_s, dp_s, carry_s,
):
    tokens = x_ref.shape[0]
    steps = tokens // SEGS
    block = 256
    f32 = jnp.float32
    for f in range(3):
        x_s[f, 0:PAD, :] = jnp.zeros((PAD, LANES), f32)
        ds_s[f, PAD + tokens : PAD + tokens + PAD, :] = jnp.zeros((PAD, LANES), f32)
    dg_s[0:tokens, :] = dg_ref[...].astype(f32)

    def gather(i, unused):
        at = pl.multiple_of(i * block, block)
        rows = lax.broadcasted_iota(jnp.int32, (block, tokens), 1)
        pick = jnp.where(src_col_ref[pl.ds(at, block), :] == rows, 1.0, 0.0).astype(jnp.bfloat16)
        got = jnp.dot(pick, x_ref[...], preferred_element_type=f32)
        for f in range(3):
            x_s[f, pl.ds(PAD + at, block), :] = got[:, f * LANES : (f + 1) * LANES]
        return unused

    lax.fori_loop(0, tokens // block, gather, 0)

    decay = [jnp.exp(-1.0 / memory_ref[m : m + 1, :]) for m in range(2)]
    norm = [jnp.sqrt(1.0 - d * d) for d in decay]
    gain = [residue_ref[m : m + 1, :] * norm[m] for m in range(2)]
    whole = [jnp.exp(-float(steps) / memory_ref[m : m + 1, :]) for m in range(2)]
    skip = skip_ref[0:1, :]
    tap = [[taps_ref[3 * f + j : 3 * f + j + 1, :] for j in range(3)] for f in range(3)]

    def at(b, shift=0):
        return pl.ds(PAD + b + shift, SEGS, stride=steps)

    def line(b):
        return pl.ds(pl.multiple_of(b * SEGS, SEGS), SEGS)

    def short(f, b, rel):
        total = tap[f][0] * x_s[f, at(b), :]
        for j in (1, 2):
            total = total + jnp.where(rel >= j, tap[f][j] * x_s[f, at(b, -j), :], 0.0)
        return total

    zero = jnp.zeros((SEGS, LANES), f32)

    def first(b, state):
        rel = rel_ref[at(b), :]
        k = short(1, b, rel)
        v = short(2, b, rel)
        drive = k * v
        k_s[line(b), :] = k
        v_s[line(b), :] = v
        drive_s[line(b), :] = drive
        return tuple(jnp.where(rel >= 1, decay[m] * state[m], 0.0) + drive for m in range(2))

    ends = lax.fori_loop(0, steps, first, (zero, zero), unroll=2)
    joined = rel_ref[at(steps - 1), :] >= steps
    for m in range(2):
        link = jnp.where(joined, whole[m], 0.0)
        carry = jnp.zeros((1, LANES), f32)
        for a in range(SEGS):
            carry_s[m, a : a + 1, :] = carry
            carry = link[a : a + 1, :] * carry + ends[m][a : a + 1, :]

    def second(b, held):
        s0, s1, r0, r1, r2 = held
        rel = rel_ref[at(b), :]
        drive = drive_s[line(b), :]
        s0 = jnp.where(rel >= 1, decay[0] * s0, 0.0) + drive
        s1 = jnp.where(rel >= 1, decay[1] * s1, 0.0) + drive
        filtered = gain[0] * s0 + gain[1] * s1 + skip * drive
        query = short(0, b, rel)
        gated_s[pl.ds(b, SEGS, stride=steps), :] = query * filtered
        dg = dg_s[pl.ds(b, SEGS, stride=steps), :]
        ds_s[0, at(b), :] = dg * filtered
        df = dg * query
        df_s[line(b), :] = df
        return (s0, s1, r0 + df * s0, r1 + df * s1, r2 + df * drive)

    held = (carry_s[0], carry_s[1], zero, zero, zero)
    held = lax.fori_loop(0, steps, second, held, unroll=2)
    gated_ref[...] = gated_s[0:tokens, :].astype(jnp.bfloat16)

    def third(i, adjoint):
        b = steps - 1 - i
        ahead = rel_ref[at(b, 1), :] >= 1
        df = df_s[line(b), :]
        return tuple(gain[m] * df + jnp.where(ahead, decay[m] * adjoint[m], 0.0) for m in range(2))

    starts = lax.fori_loop(0, steps, third, (zero, zero), unroll=2)
    joined = rel_ref[at(0, steps), :] >= steps
    for m in range(2):
        link = jnp.where(joined, whole[m], 0.0)
        carry = jnp.zeros((1, LANES), f32)
        for a in reversed(range(SEGS)):
            carry_s[m, a : a + 1, :] = carry
            carry = link[a : a + 1, :] * carry + starts[m][a : a + 1, :]

    def fourth(i, adjoint):
        b = steps - 1 - i
        ahead = rel_ref[at(b, 1), :] >= 1
        df = df_s[line(b), :]
        adjoint = tuple(
            gain[m] * df + jnp.where(ahead, decay[m] * adjoint[m], 0.0) for m in range(2)
        )
        d_drive = skip * df + adjoint[0] + adjoint[1]
        ds_s[1, at(b), :] = d_drive * v_s[line(b), :]
        ds_s[2, at(b), :] = d_drive * k_s[line(b), :]
        return adjoint

    lax.fori_loop(0, steps, fourth, (carry_s[0], carry_s[1]), unroll=2)

    def fold(value):
        return jnp.sum(value.reshape(SEGS // 8, 8, LANES), axis=0)

    def fifth(b, sums):
        sums = list(sums)
        rel = [rel_ref[at(b, j), :] for j in range(3)]
        for f in range(3):
            here = ds_s[f, at(b), :]
            d_packed = tap[f][0] * here
            sums[3 * f] = sums[3 * f] + fold(here * x_s[f, at(b), :])
            for j in (1, 2):
                d_packed = d_packed + jnp.where(rel[j] >= j, tap[f][j] * ds_s[f, at(b, j), :], 0.0)
                term = jnp.where(rel[0] >= j, here * x_s[f, at(b, -j), :], 0.0)
                sums[3 * f + j] = sums[3 * f + j] + fold(term)
            dp_s[line(b), f * LANES : (f + 1) * LANES] = d_packed.astype(jnp.bfloat16)
        return tuple(sums)

    none = jnp.zeros((8, LANES), f32)
    sums = lax.fori_loop(0, steps, fifth, (none,) * 9)
    for n in range(9):
        sums_ref[n : n + 1, :] = jnp.sum(sums[n], axis=0, keepdims=True)
    for m in range(2):
        sums_ref[9 + m : 10 + m, :] = norm[m] * jnp.sum(held[2 + m], axis=0, keepdims=True)
    sums_ref[11:12, :] = jnp.sum(held[4], axis=0, keepdims=True)
    sums_ref[12:16, :] = jnp.zeros((4, LANES), f32)

    def scatter(i, unused):
        start = pl.multiple_of(i * block, block)
        rows = lax.broadcasted_iota(jnp.int32, (block, tokens), 0) + start
        pick = jnp.where(src_row_ref[...] == rows, 1.0, 0.0).astype(jnp.bfloat16)
        got = jnp.dot(pick, dp_s[...], preferred_element_type=f32)
        d_fields_ref[pl.ds(start, block), :] = got.astype(jnp.bfloat16)
        return unused

    lax.fori_loop(0, tokens // block, scatter, 0)


def channel_part(x, dg, source, starts, taps, memory, residue, skip):
    tokens = x.shape[0]
    steps = tokens // SEGS
    rel = jnp.arange(tokens, dtype=jnp.int32) - starts
    rel = jnp.broadcast_to(jnp.pad(rel, (PAD, PAD + steps))[:, None], (tokens + 2 * PAD + steps, LANES))
    source_row = source.reshape(SEGS, steps).T.reshape(1, tokens)
    f32 = jnp.float32
    padded = tokens + 2 * PAD + steps
    return pl.pallas_call(
        channel_kernel,
        out_shape=(
            jax.ShapeDtypeStruct((tokens, LANES), jnp.bfloat16),
            jax.ShapeDtypeStruct((tokens, 3 * LANES), jnp.bfloat16),
            jax.ShapeDtypeStruct((16, LANES), f32),
        ),
        scratch_shapes=[
            pltpu.VMEM((3, padded, LANES), f32),
            pltpu.VMEM((3, padded, LANES), f32),
            pltpu.VMEM((tokens + steps, LANES), f32),
            pltpu.VMEM((tokens + steps, LANES), f32),
            pltpu.VMEM((tokens, LANES), f32),
            pltpu.VMEM((tokens, LANES), f32),
            pltpu.VMEM((tokens, LANES), f32),
            pltpu.VMEM((tokens, LANES), f32),
            pltpu.VMEM((tokens, 3 * LANES), jnp.bfloat16),
            pltpu.VMEM((2, SEGS, LANES), f32),
        ],
        compiler_params=pltpu.CompilerParams(vmem_limit_bytes=48 * 1024 * 1024),
        name="channel_part",
    )(x, dg, source[:, None], source_row, rel, taps, memory, residue, skip)


def by_channels(
    fields_in, pack_source, doc_start, short_filter, memory, residue, skip_gain, w_out, cotangent
):
    rows, _, width = fields_in.shape
    peers = lax.axis_size("seq")
    here = lax.axis_index("seq")
    tokens = rows * peers
    part = width // peers

    def exchange(shard):
        return lax.all_to_all(shard, "seq", split_axis=0, concat_axis=0, tiled=True)

    x = exchange(
        fields_in.reshape(rows, 3, peers, part).transpose(2, 0, 1, 3).reshape(peers, rows, 3 * part)
    ).reshape(tokens, 3 * part)
    ints = lax.all_gather(jnp.stack([pack_source, doc_start]), "seq", axis=1, tiled=True)
    d_gated = lax.dot_general(
        lax.all_gather(cotangent, "mp", axis=1, tiled=True),
        w_out,
        (((1,), (1,)), ((), ())),
        preferred_element_type=jnp.float32,
    ).astype(jnp.bfloat16)
    dg = exchange(d_gated.reshape(rows, peers, part).transpose(1, 0, 2)).reshape(tokens, part)

    def own(array):
        return lax.dynamic_slice_in_dim(array, here * part, part, array.ndim - 1)

    gated, d_fields, sums = channel_part(
        x,
        dg,
        ints[0],
        ints[1],
        own(short_filter).reshape(9, part),
        own(memory),
        own(residue),
        own(skip_gain).reshape(1, part),
    )
    gated = exchange(gated.reshape(peers, rows, part)).transpose(1, 0, 2).reshape(rows, width)
    d_fields = exchange(d_fields.reshape(peers, rows, 3 * part))
    d_fields = d_fields.reshape(peers, rows, 3, part).transpose(1, 2, 0, 3).reshape(rows, 3, width)
    partial_out = jnp.dot(gated, w_out, preferred_element_type=jnp.float32)
    mixed = lax.psum_scatter(partial_out, "mp", scatter_dimension=1, tiled=True).astype(
        jnp.bfloat16
    )
    sums = lax.all_gather(sums, "seq", axis=1, tiled=True)
    return (mixed, d_fields, sums[:9].reshape(3, 3, width), sums[9:11], sums[11])


def chosen(*arrays):
    rows, _, width = arrays[0].shape
    peers = lax.axis_size("seq")
    if width == LANES * peers and rows * peers <= 4096 and rows % 256 == 0:
        return by_channels(*arrays)
    return per_device(*arrays)


def solution(mesh):
    placed = (
        P("seq", None, "mp"),
        P("seq"),
        P("seq"),
        P(None, None, "mp"),
        P(None, "mp"),
        P(None, "mp"),
        P("mp"),
        P("mp", None),
        P("seq", "mp"),
    )
    return jax.shard_map(
        chosen,
        mesh=mesh,
        in_specs=placed,
        out_specs=(
            P("seq", "mp"),
            P("seq", None, "mp"),
            P(None, None, "mp"),
            P(None, "mp"),
            P("mp"),
        ),
        check_vma=False,
    )
```

profile of v0, /device:TPU:0, one launch (start us, length us, event | category | flops | bytes accessed | tf_op | source)
XLA Modules:
  0.0 228.4 jit_solution(11673045369208104563)
XLA Ops:
  7.2 0.7 all-gather.2.cloned.1.call-update
  7.9 1.7 copy.23
  9.6 1.2 copy.24
  10.9 7.3 %all-to-all-start = ((bf16[8,256,384]{1,2,0:T(8,128)(2,1)}), bf16[8,256,384]{1,2,0:T(8,128)(2,1)S(1)}, u32[]{:S(2)}, u32[]{:S(2)}) async-start(bf16[8,256,384]{1,2,0:T(8,128)(2,1)} %bitcast.2), calls=%async_computation | async-start | bytes 3145728 | tf_op jit(solution)/shard_map/all_to_all | solution.py:349
  18.1 16.8 %all-gather.2.cloned.1.call-done = bf16[256,4096]{1,0:T(8,128)(2,1)} async-done(((bf16[256,1024]{1,0:T(8,128)(2,1)}), bf16[256,4096]{1,0:T(8,128)(2,1)}) %all-gather.2.cloned.1.call-update) | async-done | bytes 2097168 | tf_op jit(solution)/shard_map/all_gather | solution.py:356
  34.9 6.4 %fusion = bf16[32,8,8,128]{3,2,1,0:T(8,128)(2,1)S(1)} fusion(bf16[256,4096]{1,0:T(8,128)(2,1)} %all-gather.2.cloned.1.call-done, bf16[1024,4096]{1,0:T(8,128)(2,1)} %param.16), kind=kOutput, calls=%fused_computation.1 | convolution fusion | flops 2147745792 | bytes 11010048 | tf_op jit(solution)/shard_map/dot_general | solution.py:355
  41.3 0.9 copy.35
  42.2 12.9 %all-to-all-done = bf16[8,256,384]{1,2,0:T(8,128)(2,1)S(1)} async-done(((bf16[8,256,384]{1,2,0:T(8,128)(2,1)}), bf16[8,256,384]{1,2,0:T(8,128)(2,1)S(1)}, u32[]{:S(2)}, u32[]{:S(2)}) %all-to-all-start) | async-done | bytes 1572896 | tf_op jit(solution)/shard_map/all_to_all | solution.py:349
  55.1 3.6 %all-to-all-start.1 = ((bf16[8,256,128]{2,1,0:T(8,128)(2,1)}), bf16[8,256,128]{2,1,0:T(8,128)(2,1)S(1)}, u32[]{:S(2)}, u32[]{:S(2)}) async-start(bf16[8,256,128]{2,1,0:T(8,128)(2,1)} %bitcast.35), calls=%async_computation.1 | async-start | bytes 1048576 | tf_op jit(solution)/shard_map/all_to_all | solution.py:349
  58.9 33.0 %all_gather.10 = s32[2,2048]{1,0:T(2,128)S(1)} all-gather(s32[2,256]{1,0:T(2,128)S(1)} %pad_add_fusion), channel_id=1, replica_groups=mesh['seq'=8,'mp'=4] {'seq'}, dimensions={1}, use_global_device_ids=true | all-gather | bytes 18432 | tf_op jit(solution)/shard_map/all_gather | solution.py:354
  92.7 0.8 dynamic-slice_bitcast_fusion.skip_ref
  93.4 0.7 constant_dynamic-slice_fusion
  94.1 1.6 copy.25
  96.0 40.3 %channel_part.1 = (bf16[2048,128]{1,0:T(8,128)(2,1)S(1)}, bf16[2048,384]{1,0:T(8,128)(2,1)S(1)}, f32[16,128]{1,0:T(8,128)S(1)}) custom-call(bf16[2048,384]{1,0:T(8,128)(2,1)} %bitcast.43, bf16[2048,128]{1,0:T(8,128)(2,1)S(1)} %bitcast.37, s32[2048,1]{1,0:T(8,128)S(1)} %copy.28.src_col_ref, s32[1,2048]{1,0:T(1,128)S(1)} %reshape.58.src_row_ref, ...), custom_call_target="tpu_custom_call" | custom-call | tf_op jit(solution)/shard_map/channel_part/pallas_call | solution.py:315
  136.3 0.8 copy-done.1
  137.1 1.2 copy.29
  138.3 12.7 %all_to_all.20 = bf16[8,256,128]{1,2,0:T(8,128)(2,1)S(1)} all-to-all(bf16[8,256,128]{1,2,0:T(8,128)(2,1)S(1)} %copy.29), channel_id=1, replica_groups=mesh['seq'=8,'mp'=4] {'seq'}, dimensions={0} | all-to-all | bytes 1048576 | tf_op jit(solution)/shard_map/all_to_all | solution.py:349
  151.1 7.7 %fusion.2 = f32[256,4096]{1,0:T(8,128)} fusion(bf16[256,1024]{0,1:T(8,128)(2,1)S(1)} %bitcast.44, bf16[1024,4096]{1,0:T(8,128)(2,1)} %param.16), kind=kOutput, calls=%fused_computation.12 | convolution fusion | flops 2147483648 | bytes 13107200 | tf_op jit(solution)/shard_map/dot_general | solution.py:379
  158.8 1.6 copy.30
  160.5 3.6 %all-to-all-start.3 = ((bf16[8,256,384]{1,2,0:T(8,128)(2,1)}), bf16[8,256,384]{1,2,0:T(8,128)(2,1)S(1)}, u32[]{:S(2)}, u32[]{:S(2)}) async-start(bf16[8,256,384]{1,2,0:T(8,128)(2,1)} %copy.30), calls=%async_computation.4 | async-start | bytes 3145728 | tf_op jit(solution)/shard_map/all_to_all | solution.py:349
  164.1 51.6 %all_gather.11 = f32[16,1024]{1,0:T(8,128)S(1)} all-gather(f32[16,128]{1,0:T(8,128)S(1)} %get-tuple-element.10), channel_id=1, replica_groups=mesh['seq'=8,'mp'=4] {'seq'}, dimensions={1}, use_global_device_ids=true | all-gather | bytes 73728 | tf_op jit(solution)/shard_map/all_gather | solution.py:383
  216.9 0.6 reshape.66
  217.7 1.7 copy.32
  219.4 2.1 convert_element_type.7
  (27 shorter events, 2.5 us)
Async XLA Ops:
  7.2 85.5 %copy-start = (f32[3,3,1024]{2,1,0:T(4,128)S(1)}, f32[3,3,1024]{2,1,0:T(4,128)}, u32[]{:S(2)}) copy-start(f32[3,3,1024]{2,1,0:T(4,128)} %param.12) | copy-start | bytes 110596
  7.2 27.7 %all-gather.2.cloned.1.call-start = ((), (), s32[]{:S(2)}) async-start(), calls=%async_computation.5 | async-start | bytes 2621440 | tf_op jit(solution)/shard_map/all_gather | solution.py:356
  10.9 44.3 %all-to-all-start = ((bf16[8,256,384]{1,2,0:T(8,128)(2,1)}), bf16[8,256,384]{1,2,0:T(8,128)(2,1)S(1)}, u32[]{:S(2)}, u32[]{:S(2)}) async-start(bf16[8,256,384]{1,2,0:T(8,128)(2,1)} %bitcast.2), calls=%async_computation | async-start | bytes 3145728 | tf_op jit(solution)/shard_map/all_to_all | solution.py:349
  41.3 17.5 %copy-start.2 = (s32[256]{0:T(256)S(1)}, s32[256]{0:T(256)}, u32[]{:S(2)}) copy-start(s32[256]{0:T(256)} %param.11) | copy-start | bytes 3076
  41.3 17.5 %copy-start.3 = (s32[256]{0:T(256)S(1)}, s32[256]{0:T(256)}, u32[]{:S(2)}) copy-start(s32[256]{0:T(256)} %param.10) | copy-start | bytes 3076
  55.1 40.6 %all-to-all-start.1 = ((bf16[8,256,128]{2,1,0:T(8,128)(2,1)}), bf16[8,256,128]{2,1,0:T(8,128)(2,1)S(1)}, u32[]{:S(2)}, u32[]{:S(2)}) async-start(bf16[8,256,128]{2,1,0:T(8,128)(2,1)} %bitcast.35), calls=%async_computation.1 | async-start | bytes 1048576 | tf_op jit(solution)/shard_map/all_to_all | solution.py:349
  58.8 160.7 %reduce-scatter.2.cloned.1.call-start = ((), (), s32[]{:S(2)}) async-start(), calls=%async_computation.6 | async-start | bytes 5242880 | tf_op jit(solution)/shard_map/reduce_scatter | solution.py:380
  136.3 0.8 copy-start.1
  160.5 57.1 %all-to-all-start.3 = ((bf16[8,256,384]{1,2,0:T(8,128)(2,1)}), bf16[8,256,384]{1,2,0:T(8,128)(2,1)S(1)}, u32[]{:S(2)}, u32[]{:S(2)}) async-start(bf16[8,256,384]{1,2,0:T(8,128)(2,1)} %copy.30), calls=%async_computation.4 | async-start | bytes 3145728 | tf_op jit(solution)/shard_map/all_to_all | solution.py:349
Sparse Core Ops, SparseCore 0:
  9.6 25.2 all-gather.1
  159.0 43.5 reduce-scatter.1
where the time goes:
time: 229 us; the launch traced here: 228 us
  blocking collectives  97.4 us (43%)
  Pallas kernels  40.3 us (18%)
  waiting for transfers between devices  30.4 us (13%)
  local copies, waits for them, and re-layouts  15.3 us (7%)
  starting transfers between devices  14.6 us (6%)
  between operations  14.2 us (6%)
  matrix products  14.1 us (6%)
    all_gather x1, blocking collectives, by_channels(): sums = lax.all_gather(sums, 'seq', axis=1, tiled=True)  51.6 us
    pallas_call x1, Pallas kernels, channel_part(): pl.pallas_call(channel_kernel, out_shape=(jax.ShapeDtypeStruct((tokens, L...  40.3 us
    all_gather x1, blocking collectives, by_channels(): lax.all_gather(jnp.stack([pack_source, doc_start]), 'seq', axis=1, tiled=...  33 us
    all_gather x1, waiting for transfers between devices, by_channels(): lax.all_gather(cotangent, 'mp', axis=1, tiled=True)  16.8 us
    all_to_all x3, starting transfers between devices, exchange(): return lax.all_to_all(shard, 'seq', split_axis=0, concat_axis=0, tiled=True)  14.5 us
    all_to_all x3, waiting for transfers between devices, exchange(): return lax.all_to_all(shard, 'seq', split_axis=0, concat_axis=0, tiled=True)  12.9 us
    all_to_all x1, blocking collectives, exchange(): return lax.all_to_all(shard, 'seq', split_axis=0, concat_axis=0, tiled=True)  12.7 us
    dot_general x1, matrix products, by_channels(): partial_out = jnp.dot(gated, w_out, preferred_element_type=jnp.float32)  7.71 us
  transfers between devices with their start and end apart: 5, of which 2 were waited for; matrix products, arithmetic and copies ran while one was open for 8% of the time, Pallas kernels for 0%

commit v1 on v0

--- a/solution.py
+++ b/solution.py
@@ -149,6 +149,7 @@
     return (mixed, d_fields, d_filter, d_residue, d_skip)
 
 
+EXTRA = 16
 PAD = 8
 SEGS = 32
 LANES = 128
@@ -156,10 +157,12 @@
 
 def channel_kernel(
     x_ref, dg_ref, src_col_ref, src_row_ref, rel_ref, taps_ref, memory_ref, residue_ref, skip_ref,
-    gated_ref, d_fields_ref, sums_ref,
-    x_s, ds_s, dg_s, gated_s, drive_s, k_s, v_s, df_s, dp_s, carry_s,
+    gated_ref, d_fields_ref,
+    x_s, ds_s, dg_s, gated_s, drive_s, k_s, v_s, df_s, dp_s, carry_s, sums_s,
 ):
-    tokens = x_ref.shape[0]
+    tokens = gated_ref.shape[0]
+    peers = d_fields_ref.shape[0]
+    share = tokens // peers
     steps = tokens // SEGS
     block = 256
     f32 = jnp.float32
@@ -170,7 +173,7 @@
 
     def gather(i, unused):
         at = pl.multiple_of(i * block, block)
-        rows = lax.broadcasted_iota(jnp.int32, (block, tokens), 1)
+        rows = lax.broadcasted_iota(jnp.int32, (block, x_ref.shape[0]), 1)
         pick = jnp.where(src_col_ref[pl.ds(at, block), :] == rows, 1.0, 0.0).astype(jnp.bfloat16)
         got = jnp.dot(pick, x_ref[...], preferred_element_type=f32)
         for f in range(3):
@@ -287,25 +290,32 @@
     none = jnp.zeros((8, LANES), f32)
     sums = lax.fori_loop(0, steps, fifth, (none,) * 9)
     for n in range(9):
-        sums_ref[n : n + 1, :] = jnp.sum(sums[n], axis=0, keepdims=True)
+        sums_s[n : n + 1, :] = jnp.sum(sums[n], axis=0, keepdims=True)
     for m in range(2):
-        sums_ref[9 + m : 10 + m, :] = norm[m] * jnp.sum(held[2 + m], axis=0, keepdims=True)
-    sums_ref[11:12, :] = jnp.sum(held[4], axis=0, keepdims=True)
-    sums_ref[12:16, :] = jnp.zeros((4, LANES), f32)
+        sums_s[9 + m : 10 + m, :] = norm[m] * jnp.sum(held[2 + m], axis=0, keepdims=True)
+    sums_s[11:12, :] = jnp.sum(held[4], axis=0, keepdims=True)
+    sums_s[12:16, :] = jnp.zeros((4, LANES), f32)
+    rest = sums_s[...]
+    for f in range(3):
+        part = rest.astype(jnp.bfloat16)
+        rest = rest - part.astype(f32)
+        for d in range(peers):
+            d_fields_ref[d, share : share + EXTRA, f * LANES : (f + 1) * LANES] = part
 
     def scatter(i, unused):
         start = pl.multiple_of(i * block, block)
         rows = lax.broadcasted_iota(jnp.int32, (block, tokens), 0) + start
         pick = jnp.where(src_row_ref[...] == rows, 1.0, 0.0).astype(jnp.bfloat16)
         got = jnp.dot(pick, dp_s[...], preferred_element_type=f32)
-        d_fields_ref[pl.ds(start, block), :] = got.astype(jnp.bfloat16)
+        d_fields_ref[i // (share // block), pl.ds(start % share, block), :] = got.astype(jnp.bfloat16)
         return unused
 
     lax.fori_loop(0, tokens // block, scatter, 0)
 
 
-def channel_part(x, dg, source, starts, taps, memory, residue, skip):
-    tokens = x.shape[0]
+def channel_part(x, dg, source, starts, taps, memory, residue, skip, peers):
+    tokens = dg.shape[0]
+    share = tokens // peers
     steps = tokens // SEGS
     rel = jnp.arange(tokens, dtype=jnp.int32) - starts
     rel = jnp.broadcast_to(jnp.pad(rel, (PAD, PAD + steps))[:, None], (tokens + 2 * PAD + steps, LANES))
@@ -316,8 +326,7 @@
         channel_kernel,
         out_shape=(
             jax.ShapeDtypeStruct((tokens, LANES), jnp.bfloat16),
-            jax.ShapeDtypeStruct((tokens, 3 * LANES), jnp.bfloat16),
-            jax.ShapeDtypeStruct((16, LANES), f32),
+            jax.ShapeDtypeStruct((peers, share + EXTRA, 3 * LANES), jnp.bfloat16),
         ),
         scratch_shapes=[
             pltpu.VMEM((3, padded, LANES), f32),
@@ -330,10 +339,11 @@
             pltpu.VMEM((tokens, LANES), f32),
             pltpu.VMEM((tokens, 3 * LANES), jnp.bfloat16),
             pltpu.VMEM((2, SEGS, LANES), f32),
+            pltpu.VMEM((EXTRA, LANES), f32),
         ],
         compiler_params=pltpu.CompilerParams(vmem_limit_bytes=48 * 1024 * 1024),
         name="channel_part",
-    )(x, dg, source[:, None], source_row, rel, taps, memory, residue, skip)
+    )(x, dg, (source + EXTRA * (source // share))[:, None], source_row, rel, taps, memory, residue, skip)
 
 
 def by_channels(
@@ -348,10 +358,15 @@
     def exchange(shard):
         return lax.all_to_all(shard, "seq", split_axis=0, concat_axis=0, tiled=True)
 
-    x = exchange(
-        fields_in.reshape(rows, 3, peers, part).transpose(2, 0, 1, 3).reshape(peers, rows, 3 * part)
-    ).reshape(tokens, 3 * part)
-    ints = lax.all_gather(jnp.stack([pack_source, doc_start]), "seq", axis=1, tiled=True)
+    fields = fields_in.reshape(rows, 3, peers, part).transpose(2, 0, 1, 3)
+    ints = jnp.concatenate([pack_source, doc_start])
+    digits = jnp.concatenate([ints // 128, ints % 128]).astype(jnp.bfloat16)
+    digits = jnp.pad(digits, (0, EXTRA * 3 * part - digits.shape[0])).reshape(1, EXTRA, 3 * part)
+    digits = jnp.broadcast_to(digits, (peers, EXTRA, 3 * part))
+    x = exchange(jnp.concatenate([fields.reshape(peers, rows, 3 * part), digits], axis=1))
+    digits = x[:, rows:].reshape(peers, EXTRA * 3 * part)[:, : 4 * rows].astype(jnp.int32)
+    ints = digits[:, : 2 * rows] * 128 + digits[:, 2 * rows :]
+    x = x.reshape(-1, 3 * part)
     d_gated = lax.dot_general(
         lax.all_gather(cotangent, "mp", axis=1, tiled=True),
         w_out,
@@ -363,31 +378,33 @@
     def own(array):
         return lax.dynamic_slice_in_dim(array, here * part, part, array.ndim - 1)
 
-    gated, d_fields, sums = channel_part(
+    gated, d_fields = channel_part(
         x,
         dg,
-        ints[0],
-        ints[1],
+        ints[:, :rows].reshape(tokens),
+        ints[:, rows:].reshape(tokens),
         own(short_filter).reshape(9, part),
         own(memory),
         own(residue),
         own(skip_gain).reshape(1, part),
+        peers,
     )
     gated = exchange(gated.reshape(peers, rows, part)).transpose(1, 0, 2).reshape(rows, width)
-    d_fields = exchange(d_fields.reshape(peers, rows, 3 * part))
-    d_fields = d_fields.reshape(peers, rows, 3, part).transpose(1, 2, 0, 3).reshape(rows, 3, width)
+    arrived = exchange(d_fields)
+    d_fields = arrived[:, :rows].reshape(peers, rows, 3, part).transpose(1, 2, 0, 3).reshape(rows, 3, width)
     partial_out = jnp.dot(gated, w_out, preferred_element_type=jnp.float32)
     mixed = lax.psum_scatter(partial_out, "mp", scatter_dimension=1, tiled=True).astype(
         jnp.bfloat16
     )
-    sums = lax.all_gather(sums, "seq", axis=1, tiled=True)
+    sums = arrived[:, rows:].reshape(peers, EXTRA, 3, part).astype(jnp.float32).sum(axis=2)
+    sums = sums.transpose(1, 0, 2).reshape(EXTRA, width)
     return (mixed, d_fields, sums[:9].reshape(3, 3, width), sums[9:11], sums[11])
 
 
 def chosen(*arrays):
     rows, _, width = arrays[0].shape
     peers = lax.axis_size("seq")
-    if width == LANES * peers and rows * peers <= 4096 and rows % 256 == 0:
+    if width == LANES * peers and rows * peers <= 4096 and rows % 256 == 0 and 4 * rows <= EXTRA * 3 * LANES:
         return by_channels(*arrays)
     return per_device(*arrays)
 

time: 229 us -> 214 us (0.934)
  blocking collectives: 97.4 us -> 60.8 us
  waiting for transfers between devices: 30.4 us -> 50.8 us
  starting transfers between devices: 14.6 us -> 11 us
    all_gather x2 -> x0, blocking collectives: 84.7 us -> none  [the longest x1 51.6 us: by_channels(): sums = lax.all_gather(sums, 'seq', axis=1, tiled=True)]
    all_to_all x1 -> x2, blocking collectives: 12.7 us -> 60.8 us  [exchange(): return lax.all_to_all(shard, 'seq', split_axis=0, concat_axis=0, tiled=True)]
    all_to_all x3 -> x2, waiting for transfers between devices: 12.9 us -> 50.1 us  [exchange(): return lax.all_to_all(shard, 'seq', split_axis=0, concat_axis=0, tiled=True)]
    all_gather x1, waiting for transfers between devices: 16.8 us -> 0.02 us  [by_channels(): lax.all_gather(cotangent, 'mp', axis=1, tiled=True)]
    all_to_all x3 -> x2, starting transfers between devices: 14.5 us -> 10.9 us  [exchange(): return lax.all_to_all(shard, 'seq', split_axis=0, concat_axis=0, tiled=True)]
    concatenate x0 -> x2, local copies, waits for them, and re-layouts: none -> 3.14 us  [the longest x1 2.45 us: by_channels(): jnp.concatenate([fields.reshape(peers, rows, 3 * part), digits], axis=1)]
    unnamed x10 -> x17, local copies, waits for them, and re-layouts: 4.26 us -> 6.58 us
  transfers between devices with their start and end apart: 5 -> 4, of which waited for: 2 -> 2; matrix products, arithmetic and copies ran while one was open for 8% -> 4% of each run, Pallas kernels for 0% -> 0%
where the time goes in v1:
time: 214 us
  blocking collectives  60.8 us (28%)
  waiting for transfers between devices  50.8 us (24%)
  Pallas kernels  40.8 us (19%)
  local copies, waits for them, and re-layouts  17.4 us (8%)
  matrix products  14.6 us (7%)
  between operations  14.3 us (7%)
  starting transfers between devices  11 us (5%)
  other arithmetic  4.16 us (2%)
    all_to_all x2, blocking collectives, exchange(): return lax.all_to_all(shard, 'seq', split_axis=0, concat_axis=0, tiled=True)  60.8 us
    all_to_all x2, waiting for transfers between devices, exchange(): return lax.all_to_all(shard, 'seq', split_axis=0, concat_axis=0, tiled=True)  50.1 us
    pallas_call x1, Pallas kernels, channel_part(): pl.pallas_call(channel_kernel, out_shape=(jax.ShapeDtypeStruct((tokens, L...  40.8 us
    all_to_all x2, starting transfers between devices, exchange(): return lax.all_to_all(shard, 'seq', split_axis=0, concat_axis=0, tiled=True)  10.9 us
    dot_general x1, matrix products, by_channels(): partial_out = jnp.dot(gated, w_out, preferred_element_type=jnp.float32)  7.72 us
    dot_general x1, matrix products, by_channels(): lax.dot_general(lax.all_gather(cotangent, 'mp', axis=1, tiled=True), w_ou...  6.89 us
    unnamed x17, local copies, waits for them, and re-layouts  6.58 us
  transfers between devices with their start and end apart: 4, of which 2 were waited for; matrix products, arithmetic and copies ran while one was open for 4% of the time, Pallas kernels for 0%

profile of v1, /device:TPU:0, one launch (start us, length us, event | category | flops | bytes accessed | tf_op | source)
XLA Modules:
  0.0 213.8 jit_solution(15678572583376104430)
XLA Ops:
  7.2 0.7 constant_dynamic-update-slice_fusion.1
  7.9 0.7 constant_dynamic-update-slice_fusion
  8.8 1.7 copy.74
  11.1 2.4 %copy.77 = bf16[8,272,384]{2,1,0:T(8,128)(2,1)} copy(bf16[8,272,384]{1,2,0:T(8,128)(2,1)S(1)} %pad_maximum_fusion) | data formatting | bytes 3342336 | tf_op jit(solution)/shard_map/concatenate | solution.py:366
  13.5 7.3 %all-to-all-start = ((bf16[8,272,384]{2,1,0:T(8,128)(2,1)}), bf16[8,272,384]{2,1,0:T(8,128)(2,1)S(1)}, u32[]{:S(2)}, u32[]{:S(2)}) async-start(bf16[8,272,384]{2,1,0:T(8,128)(2,1)} %copy.77), calls=%async_computation | async-start | bytes 3342336 | tf_op jit(solution)/shard_map/all_to_all | solution.py:359
  20.8 0.7 all-gather.2.cloned.1.call-update
  21.5 0.8 dynamic-slice_bitcast_fusion.skip_ref
  22.3 0.7 constant_dynamic-slice_fusion
  23.0 36.9 %all-to-all-done = bf16[8,272,384]{2,1,0:T(8,128)(2,1)S(1)} async-done(((bf16[8,272,384]{2,1,0:T(8,128)(2,1)}), bf16[8,272,384]{2,1,0:T(8,128)(2,1)S(1)}, u32[]{:S(2)}, u32[]{:S(2)}) %all-to-all-start) | async-done | bytes 1671200 | tf_op jit(solution)/shard_map/all_to_all | solution.py:359
  60.0 6.9 %fusion = bf16[32,8,8,128]{3,2,1,0:T(8,128)(2,1)S(1)} fusion(bf16[256,4096]{1,0:T(8,128)(2,1)} %all-gather.2.cloned.1.call-done, bf16[1024,4096]{1,0:T(8,128)(2,1)} %param.16), kind=kOutput, calls=%fused_computation.6 | convolution fusion | flops 2147745792 | bytes 11010048 | tf_op jit(solution)/shard_map/dot_general | solution.py:370
  66.9 0.9 copy.97
  67.8 3.6 %all-to-all-start.1 = ((bf16[8,256,128]{2,1,0:T(8,128)(2,1)}), bf16[8,256,128]{2,1,0:T(8,128)(2,1)S(1)}, u32[]{:S(2)}, u32[]{:S(2)}) async-start(bf16[8,256,128]{2,1,0:T(8,128)(2,1)} %bitcast.63), calls=%async_computation.1 | async-start | bytes 1048576 | tf_op jit(solution)/shard_map/all_to_all | solution.py:359
  72.8 13.2 %all-to-all-done.1 = bf16[8,256,128]{2,1,0:T(8,128)(2,1)S(1)} async-done(((bf16[8,256,128]{2,1,0:T(8,128)(2,1)}), bf16[8,256,128]{2,1,0:T(8,128)(2,1)S(1)}, u32[]{:S(2)}, u32[]{:S(2)}) %all-to-all-start.1) | async-done | bytes 524320 | tf_op jit(solution)/shard_map/all_to_all | solution.py:359
  86.4 40.8 %channel_part.1 = (bf16[2048,128]{1,0:T(8,128)(2,1)S(1)}, bf16[8,272,384]{2,1,0:T(8,128)(2,1)S(1)}) custom-call(bf16[2176,384]{1,0:T(8,128)(2,1)} %bitcast.67, bf16[2048,128]{1,0:T(8,128)(2,1)S(1)} %bitcast.65, s32[2048,1]{1,0:T(8,128)S(1)} %fusion.3.src_col_ref, s32[1,2048]{1,0:T(1,128)S(1)} %reshape.159.src_row_ref, ...), custom_call_target="tpu_custom_call" | custom-call | tf_op jit(solution)/shard_map/channel_part/pallas_call | solution.py:325
  127.2 0.8 copy-done.1
  128.0 1.2 copy.86
  129.3 18.1 %all_to_all.20 = bf16[8,256,128]{1,2,0:T(8,128)(2,1)S(1)} all-to-all(bf16[8,256,128]{1,2,0:T(8,128)(2,1)S(1)} %copy.86), channel_id=1, replica_groups=mesh['seq'=8,'mp'=4] {'seq'}, dimensions={0} | all-to-all | bytes 1048576 | tf_op jit(solution)/shard_map/all_to_all | solution.py:359
  147.4 7.7 %fusion.12 = f32[256,4096]{1,0:T(8,128)} fusion(bf16[256,1024]{0,1:T(8,128)(2,1)S(1)} %bitcast.72, bf16[1024,4096]{1,0:T(8,128)(2,1)} %param.16), kind=kOutput, calls=%fused_computation.44 | convolution fusion | flops 2147483648 | bytes 13107200 | tf_op jit(solution)/shard_map/dot_general | solution.py:395
  155.1 42.7 %all_to_all.21 = bf16[8,272,384]{2,1,0:T(8,128)(2,1)S(1)} all-to-all(bf16[8,272,384]{2,1,0:T(8,128)(2,1)S(1)} %get-tuple-element.8), channel_id=1, replica_groups=mesh['seq'=8,'mp'=4] {'seq'}, dimensions={0} | all-to-all | bytes 3342336 | tf_op jit(solution)/shard_map/all_to_all | solution.py:359
  197.8 1.2 copy-done.3
  199.2 0.8 copy.87
  200.1 1.7 copy.90
  201.9 0.9 slice_convert_fusion
  204.9 2.1 convert_element_type.20
  (44 shorter events, 5.0 us)
Async XLA Ops:
  7.2 14.3 %copy-start = (f32[3,3,1024]{2,1,0:T(4,128)S(1)}, f32[3,3,1024]{2,1,0:T(4,128)}, u32[]{:S(2)}) copy-start(f32[3,3,1024]{2,1,0:T(4,128)} %param.12) | copy-start | bytes 110596
  13.5 46.4 %all-to-all-start = ((bf16[8,272,384]{2,1,0:T(8,128)(2,1)}), bf16[8,272,384]{2,1,0:T(8,128)(2,1)S(1)}, u32[]{:S(2)}, u32[]{:S(2)}) async-start(bf16[8,272,384]{2,1,0:T(8,128)(2,1)} %copy.77), calls=%async_computation | async-start | bytes 3342336 | tf_op jit(solution)/shard_map/all_to_all | solution.py:359
  20.8 39.2 %all-gather.2.cloned.1.call-start = ((), (), s32[]{:S(2)}) async-start(), calls=%async_computation.5 | async-start | bytes 2621440 | tf_op jit(solution)/shard_map/all_gather | solution.py:371
  59.9 7.0 %copy-start.2 = (bf16[8,272,384]{2,1,0:T(8,128)(2,1)}, bf16[8,272,384]{2,1,0:T(8,128)(2,1)S(1)}, u32[]{:S(2)}) copy-start(bf16[8,272,384]{2,1,0:T(8,128)(2,1)S(1)} %all-to-all-done) | copy-start | bytes 5013508
  67.8 18.3 %all-to-all-start.1 = ((bf16[8,256,128]{2,1,0:T(8,128)(2,1)}), bf16[8,256,128]{2,1,0:T(8,128)(2,1)S(1)}, u32[]{:S(2)}, u32[]{:S(2)}) async-start(bf16[8,256,128]{2,1,0:T(8,128)(2,1)} %bitcast.63), calls=%async_computation.1 | async-start | bytes 1048576 | tf_op jit(solution)/shard_map/all_to_all | solution.py:359
  71.4 133.5 %reduce-scatter.2.cloned.1.call-start = ((), (), s32[]{:S(2)}) async-start(), calls=%async_computation.6 | async-start | bytes 5242880 | tf_op jit(solution)/shard_map/reduce_scatter | solution.py:396
  127.2 0.8 copy-start.1
  197.8 1.2 copy-start.3
Sparse Core Ops, SparseCore 0:
  23.2 24.0 all-gather.1
  155.2 43.5 reduce-scatter.1

commit v2 on v1

--- a/solution.py
+++ b/solution.py
@@ -155,21 +155,45 @@
 LANES = 128
 
 
-def channel_kernel(
-    x_ref, dg_ref, src_col_ref, src_row_ref, rel_ref, taps_ref, memory_ref, residue_ref, skip_ref,
-    gated_ref, d_fields_ref,
-    x_s, ds_s, dg_s, gated_s, drive_s, k_s, v_s, df_s, dp_s, carry_s, sums_s,
+def at(b, steps, shift=0):
+    return pl.ds(PAD + b + shift, SEGS, stride=steps)
+
+
+def line(b):
+    return pl.ds(pl.multiple_of(b * SEGS, SEGS), SEGS)
+
+
+def modes_of(memory_ref, residue_ref, steps):
+    decay = [jnp.exp(-1.0 / memory_ref[m : m + 1, :]) for m in range(2)]
+    norm = [jnp.sqrt(1.0 - d * d) for d in decay]
+    gain = [residue_ref[m : m + 1, :] * norm[m] for m in range(2)]
+    whole = [jnp.exp(-float(steps) / memory_ref[m : m + 1, :]) for m in range(2)]
+    return decay, norm, gain, whole
+
+
+def taps_of(taps_ref):
+    return [[taps_ref[3 * f + j : 3 * f + j + 1, :] for j in range(3)] for f in range(3)]
+
+
+def short_of(x_s, tap, steps, f, b, rel):
+    total = tap[f][0] * x_s[f, at(b, steps), :]
+    for j in (1, 2):
+        total = total + jnp.where(rel >= j, tap[f][j] * x_s[f, at(b, steps, -j), :], 0.0)
+    return total
+
+
+def forward_kernel(
+    x_ref, src_col_ref, rel_ref, taps_ref, memory_ref, residue_ref, skip_ref,
+    gated_ref, x_s, k_s, v_s, drive_s, filtered_s, state_s,
+    gated_s, carry_s,
 ):
     tokens = gated_ref.shape[0]
-    peers = d_fields_ref.shape[0]
-    share = tokens // peers
     steps = tokens // SEGS
     block = 256
     f32 = jnp.float32
     for f in range(3):
         x_s[f, 0:PAD, :] = jnp.zeros((PAD, LANES), f32)
-        ds_s[f, PAD + tokens : PAD + tokens + PAD, :] = jnp.zeros((PAD, LANES), f32)
-    dg_s[0:tokens, :] = dg_ref[...].astype(f32)
+        x_s[f, PAD + tokens :, :] = jnp.zeros((x_s.shape[1] - PAD - tokens, LANES), f32)
 
     def gather(i, unused):
         at = pl.multiple_of(i * block, block)
@@ -182,31 +206,16 @@
 
     lax.fori_loop(0, tokens // block, gather, 0)
 
-    decay = [jnp.exp(-1.0 / memory_ref[m : m + 1, :]) for m in range(2)]
-    norm = [jnp.sqrt(1.0 - d * d) for d in decay]
-    gain = [residue_ref[m : m + 1, :] * norm[m] for m in range(2)]
-    whole = [jnp.exp(-float(steps) / memory_ref[m : m + 1, :]) for m in range(2)]
+    decay, norm, gain, whole = modes_of(memory_ref, residue_ref, steps)
     skip = skip_ref[0:1, :]
-    tap = [[taps_ref[3 * f + j : 3 * f + j + 1, :] for j in range(3)] for f in range(3)]
-
-    def at(b, shift=0):
-        return pl.ds(PAD + b + shift, SEGS, stride=steps)
-
-    def line(b):
-        return pl.ds(pl.multiple_of(b * SEGS, SEGS), SEGS)
-
-    def short(f, b, rel):
-        total = tap[f][0] * x_s[f, at(b), :]
-        for j in (1, 2):
-            total = total + jnp.where(rel >= j, tap[f][j] * x_s[f, at(b, -j), :], 0.0)
-        return total
+    tap = taps_of(taps_ref)
 
     zero = jnp.zeros((SEGS, LANES), f32)
 
     def first(b, state):
-        rel = rel_ref[at(b), :]
-        k = short(1, b, rel)
-        v = short(2, b, rel)
+        rel = rel_ref[at(b, steps), :]
+        k = short_of(x_s, tap, steps, 1, b, rel)
+        v = short_of(x_s, tap, steps, 2, b, rel)
         drive = k * v
         k_s[line(b), :] = k
         v_s[line(b), :] = v
@@ -214,7 +223,7 @@
         return tuple(jnp.where(rel >= 1, decay[m] * state[m], 0.0) + drive for m in range(2))
 
     ends = lax.fori_loop(0, steps, first, (zero, zero), unroll=2)
-    joined = rel_ref[at(steps - 1), :] >= steps
+    joined = rel_ref[at(steps - 1, steps), :] >= steps
     for m in range(2):
         link = jnp.where(joined, whole[m], 0.0)
         carry = jnp.zeros((1, LANES), f32)
@@ -222,33 +231,56 @@
             carry_s[m, a : a + 1, :] = carry
             carry = link[a : a + 1, :] * carry + ends[m][a : a + 1, :]
 
-    def second(b, held):
-        s0, s1, r0, r1, r2 = held
-        rel = rel_ref[at(b), :]
+    def second(b, state):
+        rel = rel_ref[at(b, steps), :]
         drive = drive_s[line(b), :]
-        s0 = jnp.where(rel >= 1, decay[0] * s0, 0.0) + drive
-        s1 = jnp.where(rel >= 1, decay[1] * s1, 0.0) + drive
-        filtered = gain[0] * s0 + gain[1] * s1 + skip * drive
-        query = short(0, b, rel)
-        gated_s[pl.ds(b, SEGS, stride=steps), :] = query * filtered
+        state = tuple(jnp.where(rel >= 1, decay[m] * state[m], 0.0) + drive for m in range(2))
+        filtered = gain[0] * state[0] + gain[1] * state[1] + skip * drive
+        filtered_s[line(b), :] = filtered
+        for m in range(2):
+            state_s[m, line(b), :] = state[m]
+        gated_s[pl.ds(b, SEGS, stride=steps), :] = short_of(x_s, tap, steps, 0, b, rel) * filtered
+        return state
+
+    lax.fori_loop(0, steps, second, (carry_s[0], carry_s[1]), unroll=2)
+    gated_ref[...] = gated_s[0:tokens, :].astype(jnp.bfloat16)
+
+
+def backward_kernel(
+    dg_ref, x_s, k_s, v_s, drive_s, filtered_s, state_s,
+    src_row_ref, rel_ref, taps_ref, memory_ref, residue_ref, skip_ref,
+    d_fields_ref,
+    ds_s, dg_s, df_s, dp_s, carry_s, sums_s,
+):
+    tokens = dg_ref.shape[0]
+    peers = d_fields_ref.shape[0]
+    share = tokens // peers
+    steps = tokens // SEGS
+    block = 256
+    f32 = jnp.float32
+    for f in range(3):
+        ds_s[f, PAD + tokens : PAD + tokens + PAD, :] = jnp.zeros((PAD, LANES), f32)
+    dg_s[0:tokens, :] = dg_ref[...].astype(f32)
+    decay, norm, gain, whole = modes_of(memory_ref, residue_ref, steps)
+    skip = skip_ref[0:1, :]
+    tap = taps_of(taps_ref)
+    zero = jnp.zeros((SEGS, LANES), f32)
+
+    def third(i, held):
+        b = steps - 1 - i
+        query = short_of(x_s, tap, steps, 0, b, rel_ref[at(b, steps), :])
         dg = dg_s[pl.ds(b, SEGS, stride=steps), :]
-        ds_s[0, at(b), :] = dg * filtered
+        ds_s[0, at(b, steps), :] = dg * filtered_s[line(b), :]
         df = dg * query
         df_s[line(b), :] = df
-        return (s0, s1, r0 + df * s0, r1 + df * s1, r2 + df * drive)
-
-    held = (carry_s[0], carry_s[1], zero, zero, zero)
-    held = lax.fori_loop(0, steps, second, held, unroll=2)
-    gated_ref[...] = gated_s[0:tokens, :].astype(jnp.bfloat16)
-
-    def third(i, adjoint):
-        b = steps - 1 - i
-        ahead = rel_ref[at(b, 1), :] >= 1
-        df = df_s[line(b), :]
-        return tuple(gain[m] * df + jnp.where(ahead, decay[m] * adjoint[m], 0.0) for m in range(2))
-
-    starts = lax.fori_loop(0, steps, third, (zero, zero), unroll=2)
-    joined = rel_ref[at(0, steps), :] >= steps
+        ahead = rel_ref[at(b, steps, 1), :] >= 1
+        adjoint = [gain[m] * df + jnp.where(ahead, decay[m] * held[m], 0.0) for m in range(2)]
+        sums = [held[2 + m] + df * state_s[m, line(b), :] for m in range(2)]
+        return (*adjoint, *sums, held[4] + df * drive_s[line(b), :])
+
+    held = lax.fori_loop(0, steps, third, (zero,) * 5, unroll=2)
+    starts = held[:2]
+    joined = rel_ref[at(0, steps, steps), :] >= steps
     for m in range(2):
         link = jnp.where(joined, whole[m], 0.0)
         carry = jnp.zeros((1, LANES), f32)
@@ -258,14 +290,14 @@
 
     def fourth(i, adjoint):
         b = steps - 1 - i
-        ahead = rel_ref[at(b, 1), :] >= 1
+        ahead = rel_ref[at(b, steps, 1), :] >= 1
         df = df_s[line(b), :]
         adjoint = tuple(
             gain[m] * df + jnp.where(ahead, decay[m] * adjoint[m], 0.0) for m in range(2)
         )
         d_drive = skip * df + adjoint[0] + adjoint[1]
-        ds_s[1, at(b), :] = d_drive * v_s[line(b), :]
-        ds_s[2, at(b), :] = d_drive * k_s[line(b), :]
+        ds_s[1, at(b, steps), :] = d_drive * v_s[line(b), :]
+        ds_s[2, at(b, steps), :] = d_drive * k_s[line(b), :]
         return adjoint
 
     lax.fori_loop(0, steps, fourth, (carry_s[0], carry_s[1]), unroll=2)
@@ -275,14 +307,14 @@
 
     def fifth(b, sums):
         sums = list(sums)
-        rel = [rel_ref[at(b, j), :] for j in range(3)]
+        rel = [rel_ref[at(b, steps, j), :] for j in range(3)]
         for f in range(3):
-            here = ds_s[f, at(b), :]
+            here = ds_s[f, at(b, steps), :]
             d_packed = tap[f][0] * here
-            sums[3 * f] = sums[3 * f] + fold(here * x_s[f, at(b), :])
+            sums[3 * f] = sums[3 * f] + fold(here * x_s[f, at(b, steps), :])
             for j in (1, 2):
-                d_packed = d_packed + jnp.where(rel[j] >= j, tap[f][j] * ds_s[f, at(b, j), :], 0.0)
-                term = jnp.where(rel[0] >= j, here * x_s[f, at(b, -j), :], 0.0)
+                d_packed = d_packed + jnp.where(rel[j] >= j, tap[f][j] * ds_s[f, at(b, steps, j), :], 0.0)
+                term = jnp.where(rel[0] >= j, here * x_s[f, at(b, steps, -j), :], 0.0)
                 sums[3 * f + j] = sums[3 * f + j] + fold(term)
             dp_s[line(b), f * LANES : (f + 1) * LANES] = d_packed.astype(jnp.bfloat16)
         return tuple(sums)
@@ -313,37 +345,57 @@
     lax.fori_loop(0, tokens // block, scatter, 0)
 
 
-def channel_part(x, dg, source, starts, taps, memory, residue, skip, peers):
-    tokens = dg.shape[0]
-    share = tokens // peers
+def plan(tokens):
     steps = tokens // SEGS
-    rel = jnp.arange(tokens, dtype=jnp.int32) - starts
-    rel = jnp.broadcast_to(jnp.pad(rel, (PAD, PAD + steps))[:, None], (tokens + 2 * PAD + steps, LANES))
-    source_row = source.reshape(SEGS, steps).T.reshape(1, tokens)
+    padded = tokens + 2 * PAD + steps
+    return steps, padded
+
+
+def forward_part(x, source, rel, taps, memory, residue, skip, tokens, share):
+    steps, padded = plan(tokens)
     f32 = jnp.float32
-    padded = tokens + 2 * PAD + steps
+    column = jax.ShapeDtypeStruct((tokens, LANES), f32)
     return pl.pallas_call(
-        channel_kernel,
+        forward_kernel,
         out_shape=(
             jax.ShapeDtypeStruct((tokens, LANES), jnp.bfloat16),
-            jax.ShapeDtypeStruct((peers, share + EXTRA, 3 * LANES), jnp.bfloat16),
+            jax.ShapeDtypeStruct((3, padded, LANES), f32),
+            column,
+            column,
+            column,
+            column,
+            jax.ShapeDtypeStruct((2, tokens, LANES), f32),
         ),
         scratch_shapes=[
-            pltpu.VMEM((3, padded, LANES), f32),
+            pltpu.VMEM((tokens + steps, LANES), f32),
+            pltpu.VMEM((2, SEGS, LANES), f32),
+        ],
+        compiler_params=pltpu.CompilerParams(vmem_limit_bytes=32 * 1024 * 1024),
+        cost_estimate=pl.CostEstimate(flops=20_000_000_000, bytes_accessed=16_000_000, transcendentals=0),
+        name="forward_part",
+    )(x, (source + EXTRA * (source // share))[:, None], rel, taps, memory, residue, skip)
+
+
+def backward_part(dg, kept, source, rel, taps, memory, residue, skip, peers):
+    tokens = dg.shape[0]
+    steps, padded = plan(tokens)
+    f32 = jnp.float32
+    source_row = source.reshape(SEGS, steps).T.reshape(1, tokens)
+    return pl.pallas_call(
+        backward_kernel,
+        out_shape=jax.ShapeDtypeStruct((peers, tokens // peers + EXTRA, 3 * LANES), jnp.bfloat16),
+        scratch_shapes=[
             pltpu.VMEM((3, padded, LANES), f32),
             pltpu.VMEM((tokens + steps, LANES), f32),
-            pltpu.VMEM((tokens + steps, LANES), f32),
-            pltpu.VMEM((tokens, LANES), f32),
-            pltpu.VMEM((tokens, LANES), f32),
-            pltpu.VMEM((tokens, LANES), f32),
             pltpu.VMEM((tokens, LANES), f32),
             pltpu.VMEM((tokens, 3 * LANES), jnp.bfloat16),
             pltpu.VMEM((2, SEGS, LANES), f32),
             pltpu.VMEM((EXTRA, LANES), f32),
         ],
-        compiler_params=pltpu.CompilerParams(vmem_limit_bytes=48 * 1024 * 1024),
-        name="channel_part",
-    )(x, dg, (source + EXTRA * (source // share))[:, None], source_row, rel, taps, memory, residue, skip)
+        compiler_params=pltpu.CompilerParams(vmem_limit_bytes=32 * 1024 * 1024),
+        cost_estimate=pl.CostEstimate(flops=20_000_000_000, bytes_accessed=16_000_000, transcendentals=0),
+        name="backward_part",
+    )(dg, *kept, source_row, rel, taps, memory, residue, skip)
 
 
 def by_channels(
@@ -373,23 +425,26 @@
         (((1,), (1,)), ((), ())),
         preferred_element_type=jnp.float32,
     ).astype(jnp.bfloat16)
-    dg = exchange(d_gated.reshape(rows, peers, part).transpose(1, 0, 2)).reshape(tokens, part)
+    d_gated = d_gated.reshape(rows, peers, part).transpose(1, 0, 2)
 
     def own(array):
         return lax.dynamic_slice_in_dim(array, here * part, part, array.ndim - 1)
 
-    gated, d_fields = channel_part(
-        x,
-        dg,
-        ints[:, :rows].reshape(tokens),
-        ints[:, rows:].reshape(tokens),
+    source = ints[:, :rows].reshape(tokens)
+    steps, padded = plan(tokens)
+    rel = jnp.arange(tokens, dtype=jnp.int32) - ints[:, rows:].reshape(tokens)
+    rel = jnp.broadcast_to(jnp.pad(rel, (PAD, PAD + steps))[:, None], (padded, LANES))
+    weights = (
         own(short_filter).reshape(9, part),
         own(memory),
         own(residue),
         own(skip_gain).reshape(1, part),
-        peers,
-    )
-    gated = exchange(gated.reshape(peers, rows, part)).transpose(1, 0, 2).reshape(rows, width)
+    )
+    gated, *kept = forward_part(x, source, rel, *weights, tokens, rows)
+    both = exchange(jnp.concatenate([d_gated, gated.reshape(peers, rows, part)], axis=1))
+    dg = both[:, :rows].reshape(tokens, part)
+    d_fields = backward_part(dg, kept, source, rel, *weights, peers)
+    gated = both[:, rows:].transpose(1, 0, 2).reshape(rows, width)
     arrived = exchange(d_fields)
     d_fields = arrived[:, :rows].reshape(peers, rows, 3, part).transpose(1, 2, 0, 3).reshape(rows, 3, width)
     partial_out = jnp.dot(gated, w_out, preferred_element_type=jnp.float32)

time: 214 us -> 226 us (1.056)
  local copies, waits for them, and re-layouts: 17.4 us -> 33.7 us
  waiting for transfers between devices: 50.8 us -> 37.5 us
  blocking collectives: 60.8 us -> 71.5 us
  starting transfers between devices: 11 us -> 7.33 us
  Pallas kernels: 40.8 us -> 43.4 us
    unnamed x17 -> x34, local copies, waits for them, and re-layouts: 6.58 us -> 21 us
    all_to_all x2 -> x1, waiting for transfers between devices: 50.1 us -> 36.8 us  [exchange(): return lax.all_to_all(shard, 'seq', split_axis=0, concat_axis=0, tiled=True)]
    all_to_all x2, blocking collectives: 60.8 us -> 71.5 us  [exchange(): return lax.all_to_all(shard, 'seq', split_axis=0, concat_axis=0, tiled=True)]
    all_to_all x2 -> x1, starting transfers between devices: 10.9 us -> 7.25 us  [exchange(): return lax.all_to_all(shard, 'seq', split_axis=0, concat_axis=0, tiled=True)]
    pallas_call x1 -> x2, Pallas kernels: 40.8 us -> 43.4 us  [the longest x1 29.1 us: backward_part(): pl.pallas_call(backward_kernel, out_shape=jax.ShapeDtypeStruct((peers, to...]
  transfers between devices with their start and end apart: 4 -> 3, of which waited for: 2 -> 1; matrix products, arithmetic and copies ran while one was open for 4% -> 6% of each run, Pallas kernels for 0% -> 19%
where the time goes in v2:
time: 226 us; the launch traced here: 225 us
  blocking collectives  71.5 us (32%)
  Pallas kernels  43.4 us (19%)
  waiting for transfers between devices  37.5 us (17%)
  local copies, waits for them, and re-layouts  33.7 us (15%)
  between operations  14.3 us (6%)
  matrix products  14.1 us (6%)
  starting transfers between devices  7.33 us (3%)
  other arithmetic  3.35 us (1%)
    all_to_all x2, blocking collectives, exchange(): return lax.all_to_all(shard, 'seq', split_axis=0, concat_axis=0, tiled=True)  71.5 us
    all_to_all x1, waiting for transfers between devices, exchange(): return lax.all_to_all(shard, 'seq', split_axis=0, concat_axis=0, tiled=True)  36.8 us
    pallas_call x1, Pallas kernels, backward_part(): pl.pallas_call(backward_kernel, out_shape=jax.ShapeDtypeStruct((peers, to...  29.1 us
    unnamed x34, local copies, waits for them, and re-layouts  21 us
    pallas_call x1, Pallas kernels, forward_part(): pl.pallas_call(forward_kernel, out_shape=(jax.ShapeDtypeStruct((tokens, L...  14.3 us
    dot_general x1, matrix products, by_channels(): partial_out = jnp.dot(gated, w_out, preferred_element_type=jnp.float32)  7.72 us
    all_to_all x1, starting transfers between devices, exchange(): return lax.all_to_all(shard, 'seq', split_axis=0, concat_axis=0, tiled=True)  7.25 us
    dot_general x1, matrix products, by_channels(): lax.dot_general(lax.all_gather(cotangent, 'mp', axis=1, tiled=True), w_ou...  6.38 us
  transfers between devices with their start and end apart: 3, of which 1 were waited for; matrix products, arithmetic and copies ran while one was open for 6% of the time, Pallas kernels for 19%

profile of v2, /device:TPU:0, one launch (start us, length us, event | category | flops | bytes accessed | tf_op | source)
XLA Modules:
  0.0 225.3 jit_solution(6301268067731748926)
XLA Ops:
  8.8 1.7 copy.79
  11.1 2.4 %copy.82 = bf16[8,272,384]{2,1,0:T(8,128)(2,1)} copy(bf16[8,272,384]{1,2,0:T(8,128)(2,1)S(1)} %pad_maximum_fusion) | data formatting | bytes 3342336 | tf_op jit(solution)/shard_map/concatenate | solution.py:418
  13.5 7.3 %all-to-all-start = ((bf16[8,272,384]{2,1,0:T(8,128)(2,1)}), bf16[8,272,384]{2,1,0:T(8,128)(2,1)S(1)}, u32[]{:S(2)}, u32[]{:S(2)}) async-start(bf16[8,272,384]{2,1,0:T(8,128)(2,1)} %copy.82), calls=%async_computation | async-start | bytes 3342336 | tf_op jit(solution)/shard_map/all_to_all | solution.py:411
  23.0 36.8 %all-to-all-done = bf16[8,272,384]{2,1,0:T(8,128)(2,1)S(1)} async-done(((bf16[8,272,384]{2,1,0:T(8,128)(2,1)}), bf16[8,272,384]{2,1,0:T(8,128)(2,1)S(1)}, u32[]{:S(2)}, u32[]{:S(2)}) %all-to-all-start) | async-done | bytes 1671200 | tf_op jit(solution)/shard_map/all_to_all | solution.py:411
  61.4 14.3 %forward_part.1 = (bf16[2048,128]{1,0:T(8,128)(2,1)S(1)}, f32[3,2128,128]{2,1,0:T(8,128)S(1)}, f32[2048,128]{1,0:T(8,128)S(1)}, f32[2048,128]{1,0:T(8,128)S(1)},...) custom-call(bf16[2176,384]{1,0:T(8,128)(2,1)S(1)} %bitcast.60, ...), custom_call_target="tpu_custom_call" | custom-call | flops 20000000000 | bytes 16000000 | tf_op jit(solution)/shard_map/forward_part/pallas_call | solution.py:358
  75.7 1.7 copy-done.1
  77.4 1.4 copy-done.3
  80.8 1.0 copy-done.9
  81.8 1.0 copy-done.11
  83.1 6.4 %convolution_convert_fusion = bf16[256,1024]{1,0:T(8,128)(2,1)S(1)} fusion(bf16[256,4096]{1,0:T(8,128)(2,1)} %all-gather.2.cloned.1.call-done, bf16[1024,4096]{1,0:T(8,128)(2,1)} %param.16), kind=kOutput, calls=%fused_computation.5 | convolution fusion | flops 2147745792 | bytes 11010048 | tf_op jit(solution)/shard_map/dot_general | solution.py:422
  89.7 29.3 %all_to_all.15 = bf16[8,512,128]{1,2,0:T(8,128)(2,1)S(1)} all-to-all(bf16[8,512,128]{1,2,0:T(8,128)(2,1)S(1)} %pad_maximum_fusion.1), channel_id=1, replica_groups=mesh['seq'=8,'mp'=4] {'seq'}, dimensions={0} | all-to-all | bytes 2097152 | tf_op jit(solution)/shard_map/all_to_all | solution.py:411
  119.2 7.7 %fusion.13 = f32[256,4096]{1,0:T(8,128)} fusion(bf16[256,1024]{0,1:T(8,128)(2,1)S(1)} %bitcast.67, bf16[1024,4096]{1,0:T(8,128)(2,1)} %param.16), kind=kOutput, calls=%fused_computation.45 | convolution fusion | flops 2147483648 | bytes 13107200 | tf_op jit(solution)/shard_map/dot_general | solution.py:450
  128.1 1.9 copy-done.2
  130.0 1.7 copy-done.4
  131.8 1.2 copy-done.8
  133.0 1.5 copy-done.10
  134.5 1.5 copy-done.12
  135.9 29.1 %backward_part.1 = bf16[8,272,384]{2,1,0:T(8,128)(2,1)S(1)} custom-call(bf16[2048,128]{1,0:T(8,128)(2,1)S(1)} %bitcast.61, f32[3,2128,128]{2,1,0:T(8,128)S(1)} %copy-done.2, f32[2048,128]{1,0:T(8,128)S(1)} %copy-done.6, f32[2048,128]{1,0:T(8,128)S(1)} %copy-done.8, f32[2048,128]{1,0:T(8,128)S(1)} %copy-done.10, f32[2048,128]{1,0:T(8,128)S(1)} %copy-done.12, ...), custom_call_target="tpu_custom_call" | custom-call | flops 20000000000 | bytes 16000000 | tf_op jit(solution)/shard_map/backward_part/pallas_call | solution.py:384
  165.1 42.2 %all_to_all.16 = bf16[8,272,384]{2,1,0:T(8,128)(2,1)S(1)} all-to-all(bf16[8,272,384]{2,1,0:T(8,128)(2,1)S(1)} %backward_part.1), channel_id=1, replica_groups=mesh['seq'=8,'mp'=4] {'seq'}, dimensions={0} | all-to-all | bytes 3342336 | tf_op jit(solution)/shard_map/all_to_all | solution.py:411
  207.3 1.3 slice.66
  208.6 1.7 copy.92
  210.3 1.3 copy.93
  211.6 2.6 %copy.95 = bf16[256,3,1024]{2,0,1:T(8,128)(2,1)} copy(bf16[256,3,1024]{0,2,1:T(8,128)(2,1)} %bitcast.64) | data formatting | bytes 3145728
  216.3 2.1 convert_element_type.20
  (64 shorter events, 11.7 us)
Async XLA Ops:
  7.2 14.4 %copy-start = (f32[3,3,1024]{2,1,0:T(4,128)S(1)}, f32[3,3,1024]{2,1,0:T(4,128)}, u32[]{:S(2)}) copy-start(f32[3,3,1024]{2,1,0:T(4,128)} %param.12) | copy-start | bytes 110596
  13.5 46.4 %all-to-all-start = ((bf16[8,272,384]{2,1,0:T(8,128)(2,1)}), bf16[8,272,384]{2,1,0:T(8,128)(2,1)S(1)}, u32[]{:S(2)}, u32[]{:S(2)}) async-start(bf16[8,272,384]{2,1,0:T(8,128)(2,1)} %copy.82), calls=%async_computation | async-start | bytes 3342336 | tf_op jit(solution)/shard_map/all_to_all | solution.py:411
  20.8 62.3 %all-gather.2.cloned.1.call-start = ((), (), s32[]{:S(2)}) async-start(), calls=%async_computation.4 | async-start | bytes 2621440 | tf_op jit(solution)/shard_map/all_gather | solution.py:423
  21.5 194.8 %reduce-scatter.2.cloned.1.call-start = ((), (), s32[]{:S(2)}) async-start(), calls=%async_computation.5 | async-start | bytes 5242880 | tf_op jit(solution)/shard_map/reduce_scatter | solution.py:451
  75.7 1.7 copy-start.1
  77.4 1.4 copy-start.3
  78.8 1.0 copy-start.5
  79.8 1.0 copy-start.7
  80.8 1.0 copy-start.9
  81.8 1.0 copy-start.11
  126.9 1.2 copy-start.6
  128.1 1.9 copy-start.2
  130.0 1.7 copy-start.4
  131.8 1.3 copy-start.8
  133.0 1.5 copy-start.10
  134.5 1.5 copy-start.12
Sparse Core Ops, SparseCore 0:
  23.2 24.0 all-gather.1
  127.0 43.5 reduce-scatter.1

commit v3 on v1

--- a/solution.py
+++ b/solution.py
@@ -213,7 +213,7 @@
         drive_s[line(b), :] = drive
         return tuple(jnp.where(rel >= 1, decay[m] * state[m], 0.0) + drive for m in range(2))
 
-    ends = lax.fori_loop(0, steps, first, (zero, zero), unroll=2)
+    ends = lax.fori_loop(0, steps, first, (zero, zero), unroll=4)
     joined = rel_ref[at(steps - 1), :] >= steps
     for m in range(2):
         link = jnp.where(joined, whole[m], 0.0)
@@ -238,7 +238,7 @@
         return (s0, s1, r0 + df * s0, r1 + df * s1, r2 + df * drive)
 
     held = (carry_s[0], carry_s[1], zero, zero, zero)
-    held = lax.fori_loop(0, steps, second, held, unroll=2)
+    held = lax.fori_loop(0, steps, second, held, unroll=4)
     gated_ref[...] = gated_s[0:tokens, :].astype(jnp.bfloat16)
 
     def third(i, adjoint):
@@ -247,7 +247,7 @@
         df = df_s[line(b), :]
         return tuple(gain[m] * df + jnp.where(ahead, decay[m] * adjoint[m], 0.0) for m in range(2))
 
-    starts = lax.fori_loop(0, steps, third, (zero, zero), unroll=2)
+    starts = lax.fori_loop(0, steps, third, (zero, zero), unroll=4)
     joined = rel_ref[at(0, steps), :] >= steps
     for m in range(2):
         link = jnp.where(joined, whole[m], 0.0)
@@ -268,7 +268,7 @@
         ds_s[2, at(b), :] = d_drive * k_s[line(b), :]
         return adjoint
 
-    lax.fori_loop(0, steps, fourth, (carry_s[0], carry_s[1]), unroll=2)
+    lax.fori_loop(0, steps, fourth, (carry_s[0], carry_s[1]), unroll=4)
 
     def fold(value):
         return jnp.sum(value.reshape(SEGS // 8, 8, LANES), axis=0)
@@ -288,7 +288,7 @@
         return tuple(sums)
 
     none = jnp.zeros((8, LANES), f32)
-    sums = lax.fori_loop(0, steps, fifth, (none,) * 9)
+    sums = lax.fori_loop(0, steps, fifth, (none,) * 9, unroll=2)
     for n in range(9):
         sums_s[n : n + 1, :] = jnp.sum(sums[n], axis=0, keepdims=True)
     for m in range(2):

time: 214 us -> 212 us (level)
  Pallas kernels: 40.8 us -> 38.4 us
    pallas_call x1, Pallas kernels: 40.8 us -> 38.4 us  [channel_part(): pl.pallas_call(channel_kernel, out_shape=(jax.ShapeDtypeStruct((tokens, L...]
where the time goes in v3:
time: 212 us; the launch traced here: 211 us
  blocking collectives  60.8 us (29%)
  waiting for transfers between devices  50.8 us (24%)
  Pallas kernels  38.4 us (18%)
  local copies, waits for them, and re-layouts  17.4 us (8%)
  matrix products  14.6 us (7%)
  between operations  14.3 us (7%)
  starting transfers between devices  11 us (5%)
  other arithmetic  4.16 us (2%)
    all_to_all x2, blocking collectives, exchange(): return lax.all_to_all(shard, 'seq', split_axis=0, concat_axis=0, tiled=True)  60.8 us
    all_to_all x2, waiting for transfers between devices, exchange(): return lax.all_to_all(shard, 'seq', split_axis=0, concat_axis=0, tiled=True)  50.1 us
    pallas_call x1, Pallas kernels, channel_part(): pl.pallas_call(channel_kernel, out_shape=(jax.ShapeDtypeStruct((tokens, L...  38.4 us
    all_to_all x2, starting transfers between devices, exchange(): return lax.all_to_all(shard, 'seq', split_axis=0, concat_axis=0, tiled=True)  10.9 us
    dot_general x1, matrix products, by_channels(): partial_out = jnp.dot(gated, w_out, preferred_element_type=jnp.float32)  7.72 us
    dot_general x1, matrix products, by_channels(): lax.dot_general(lax.all_gather(cotangent, 'mp', axis=1, tiled=True), w_ou...  6.89 us
    unnamed x17, local copies, waits for them, and re-layouts  6.58 us
  transfers between devices with their start and end apart: 4, of which 2 were waited for; matrix products, arithmetic and copies ran while one was open for 4% of the time, Pallas kernels for 0%

profile of v3, /device:TPU:0, one launch (start us, length us, event | category | flops | bytes accessed | tf_op | source)
XLA Modules:
  0.0 211.5 jit_solution(15182692038747903825)
XLA Ops:
  7.2 0.7 constant_dynamic-update-slice_fusion.1
  7.9 0.7 constant_dynamic-update-slice_fusion
  8.8 1.7 copy.74
  11.1 2.4 %copy.77 = bf16[8,272,384]{2,1,0:T(8,128)(2,1)} copy(bf16[8,272,384]{1,2,0:T(8,128)(2,1)S(1)} %pad_maximum_fusion) | data formatting | bytes 3342336 | tf_op jit(solution)/shard_map/concatenate | solution.py:366
  13.5 7.3 %all-to-all-start = ((bf16[8,272,384]{2,1,0:T(8,128)(2,1)}), bf16[8,272,384]{2,1,0:T(8,128)(2,1)S(1)}, u32[]{:S(2)}, u32[]{:S(2)}) async-start(bf16[8,272,384]{2,1,0:T(8,128)(2,1)} %copy.77), calls=%async_computation | async-start | bytes 3342336 | tf_op jit(solution)/shard_map/all_to_all | solution.py:359
  20.8 0.7 all-gather.2.cloned.1.call-update
  21.5 0.8 dynamic-slice_bitcast_fusion.skip_ref
  22.3 0.7 constant_dynamic-slice_fusion
  23.0 36.9 %all-to-all-done = bf16[8,272,384]{2,1,0:T(8,128)(2,1)S(1)} async-done(((bf16[8,272,384]{2,1,0:T(8,128)(2,1)}), bf16[8,272,384]{2,1,0:T(8,128)(2,1)S(1)}, u32[]{:S(2)}, u32[]{:S(2)}) %all-to-all-start) | async-done | bytes 1671200 | tf_op jit(solution)/shard_map/all_to_all | solution.py:359
  60.0 6.9 %fusion = bf16[32,8,8,128]{3,2,1,0:T(8,128)(2,1)S(1)} fusion(bf16[256,4096]{1,0:T(8,128)(2,1)} %all-gather.2.cloned.1.call-done, bf16[1024,4096]{1,0:T(8,128)(2,1)} %param.16), kind=kOutput, calls=%fused_computation.6 | convolution fusion | flops 2147745792 | bytes 11010048 | tf_op jit(solution)/shard_map/dot_general | solution.py:370
  66.9 0.9 copy.97
  67.8 3.6 %all-to-all-start.1 = ((bf16[8,256,128]{2,1,0:T(8,128)(2,1)}), bf16[8,256,128]{2,1,0:T(8,128)(2,1)S(1)}, u32[]{:S(2)}, u32[]{:S(2)}) async-start(bf16[8,256,128]{2,1,0:T(8,128)(2,1)} %bitcast.63), calls=%async_computation.1 | async-start | bytes 1048576 | tf_op jit(solution)/shard_map/all_to_all | solution.py:359
  72.8 13.2 %all-to-all-done.1 = bf16[8,256,128]{2,1,0:T(8,128)(2,1)S(1)} async-done(((bf16[8,256,128]{2,1,0:T(8,128)(2,1)}), bf16[8,256,128]{2,1,0:T(8,128)(2,1)S(1)}, u32[]{:S(2)}, u32[]{:S(2)}) %all-to-all-start.1) | async-done | bytes 524320 | tf_op jit(solution)/shard_map/all_to_all | solution.py:359
  86.4 38.4 %channel_part.1 = (bf16[2048,128]{1,0:T(8,128)(2,1)S(1)}, bf16[8,272,384]{2,1,0:T(8,128)(2,1)S(1)}) custom-call(bf16[2176,384]{1,0:T(8,128)(2,1)} %bitcast.67, bf16[2048,128]{1,0:T(8,128)(2,1)S(1)} %bitcast.65, s32[2048,1]{1,0:T(8,128)S(1)} %fusion.3.src_col_ref, s32[1,2048]{1,0:T(1,128)S(1)} %reshape.159.src_row_ref, ...), custom_call_target="tpu_custom_call" | custom-call | tf_op jit(solution)/shard_map/channel_part/pallas_call | solution.py:325
  124.9 0.8 copy-done.1
  125.7 1.2 copy.86
  126.9 18.1 %all_to_all.20 = bf16[8,256,128]{1,2,0:T(8,128)(2,1)S(1)} all-to-all(bf16[8,256,128]{1,2,0:T(8,128)(2,1)S(1)} %copy.86), channel_id=1, replica_groups=mesh['seq'=8,'mp'=4] {'seq'}, dimensions={0} | all-to-all | bytes 1048576 | tf_op jit(solution)/shard_map/all_to_all | solution.py:359
  145.0 7.7 %fusion.12 = f32[256,4096]{1,0:T(8,128)} fusion(bf16[256,1024]{0,1:T(8,128)(2,1)S(1)} %bitcast.72, bf16[1024,4096]{1,0:T(8,128)(2,1)} %param.16), kind=kOutput, calls=%fused_computation.44 | convolution fusion | flops 2147483648 | bytes 13107200 | tf_op jit(solution)/shard_map/dot_general | solution.py:395
  152.8 42.7 %all_to_all.21 = bf16[8,272,384]{2,1,0:T(8,128)(2,1)S(1)} all-to-all(bf16[8,272,384]{2,1,0:T(8,128)(2,1)S(1)} %get-tuple-element.8), channel_id=1, replica_groups=mesh['seq'=8,'mp'=4] {'seq'}, dimensions={0} | all-to-all | bytes 3342336 | tf_op jit(solution)/shard_map/all_to_all | solution.py:359
  195.5 1.2 copy-done.3
  196.8 0.8 copy.87
  197.8 1.7 copy.90
  199.5 0.9 slice_convert_fusion
  202.5 2.1 convert_element_type.20
  (44 shorter events, 5.0 us)
Async XLA Ops:
  7.2 14.3 %copy-start = (f32[3,3,1024]{2,1,0:T(4,128)S(1)}, f32[3,3,1024]{2,1,0:T(4,128)}, u32[]{:S(2)}) copy-start(f32[3,3,1024]{2,1,0:T(4,128)} %param.12) | copy-start | bytes 110596
  13.5 46.4 %all-to-all-start = ((bf16[8,272,384]{2,1,0:T(8,128)(2,1)}), bf16[8,272,384]{2,1,0:T(8,128)(2,1)S(1)}, u32[]{:S(2)}, u32[]{:S(2)}) async-start(bf16[8,272,384]{2,1,0:T(8,128)(2,1)} %copy.77), calls=%async_computation | async-start | bytes 3342336 | tf_op jit(solution)/shard_map/all_to_all | solution.py:359
  20.8 39.2 %all-gather.2.cloned.1.call-start = ((), (), s32[]{:S(2)}) async-start(), calls=%async_computation.5 | async-start | bytes 2621440 | tf_op jit(solution)/shard_map/all_gather | solution.py:371
  59.9 7.0 %copy-start.2 = (bf16[8,272,384]{2,1,0:T(8,128)(2,1)}, bf16[8,272,384]{2,1,0:T(8,128)(2,1)S(1)}, u32[]{:S(2)}) copy-start(bf16[8,272,384]{2,1,0:T(8,128)(2,1)S(1)} %all-to-all-done) | copy-start | bytes 5013508
  67.8 18.3 %all-to-all-start.1 = ((bf16[8,256,128]{2,1,0:T(8,128)(2,1)}), bf16[8,256,128]{2,1,0:T(8,128)(2,1)S(1)}, u32[]{:S(2)}, u32[]{:S(2)}) async-start(bf16[8,256,128]{2,1,0:T(8,128)(2,1)} %bitcast.63), calls=%async_computation.1 | async-start | bytes 1048576 | tf_op jit(solution)/shard_map/all_to_all | solution.py:359
  71.4 131.1 %reduce-scatter.2.cloned.1.call-start = ((), (), s32[]{:S(2)}) async-start(), calls=%async_computation.6 | async-start | bytes 5242880 | tf_op jit(solution)/shard_map/reduce_scatter | solution.py:396
  124.9 0.8 copy-start.1
  195.5 1.2 copy-start.3
Sparse Core Ops, SparseCore 0:
  23.2 24.0 all-gather.1
  152.9 43.5 reduce-scatter.1
